TPU v7x, 256 devices: a whole 4x4x8 slice. The times are simulated.
256 devices in a mesh: dp: 16 (over y, x_lo, core), tensor: 16 (over z, x_hi).
Axes of the slice: x: 4 (x_hi: 2, x_lo: 2; x = x_hi * 2 + x_lo), y: 4, z: 8, core: 2. Of those that a mesh axis runs over, the one named last changes fastest.
Arguments:
- inputs: bfloat16 [2048, 4096], P('dp', 'tensor'), may hold values from -6 to 6
- gate_blocks: bfloat16 [16, 112, 128, 128], P('dp', 'tensor'), may hold values from -0.125 to 0.125
- up_blocks: bfloat16 [16, 112, 128, 128], P('dp', 'tensor'), may hold values from -0.125 to 0.125
- block_mask: int32 [32, 112], P(None, 'tensor'), may hold values from 0 to 1, as said below
- grad_hidden: bfloat16 [2048, 14336], P('dp', 'tensor'), may hold values from -6 to 6
Outputs:
- hidden: bfloat16 [2048, 14336], P('dp', 'tensor')
- grad_inputs: bfloat16 [2048, 4096], P('dp', 'tensor')
- grad_gate_blocks: bfloat16 [16, 112, 128, 128], P('dp', 'tensor')
- grad_up_blocks: bfloat16 [16, 112, 128, 128], P('dp', 'tensor')
Inputs may be any that keep to these rules, and one draw needn't show every extreme that they name: Every column of block_mask holds exactly 16 ones; the number of ones in a row differs from row to row and may be anything from 0 to 112.
All inputs are finite; a program needn't handle non-finite values.
Results may differ from a plain program's by a relative error of at most 0.023.
Values may be sent and summed in bfloat16 or wider, within the bound.
A program may use at most 128 MiB of HBM per device.

v0:
```python
import math
import jax
import jax.numpy as jnp
from jax import lax
from jax.sharding import PartitionSpec as P


def tables(block_mask, keep_total):
    row_rank = jnp.cumsum(block_mask, axis=0) - 1
    levels = jnp.arange(keep_total, dtype=jnp.int32)
    chosen = (block_mask[None] == 1) & (row_rank[None] == levels[:, None, None])
    row_ids = jnp.arange(block_mask.shape[0], dtype=jnp.int32)
    row_index = jnp.sum(jnp.where(chosen, row_ids[None, :, None], 0), axis=1)
    selector = jnp.transpose(chosen, (0, 2, 1)).astype(jnp.float32)
    return (row_index, selector)


def per_device(inputs, gate_blocks, up_blocks, block_mask, grad_hidden):
    tok_rows = inputs.shape[0]
    keep_total = gate_blocks.shape[0] * lax.axis_size("dp")
    col_local = gate_blocks.shape[1]
    side = gate_blocks.shape[2]
    row_index, selector = tables(block_mask, keep_total)
    whole = lax.all_gather(inputs, "tensor", axis=1, tiled=True)
    row_blocks = whole.shape[1] // side
    blocks = whole.reshape(tok_rows, row_blocks, side)
    pieces = (
        lax.all_gather(gate_blocks, "dp", axis=0, tiled=True),
        lax.all_gather(up_blocks, "dp", axis=0, tiled=True),
    )
    rows_here = row_index
    taken = jnp.take(blocks, rows_here, axis=1)
    gate_acc = jnp.einsum("tkcj,kcjh->tch", taken, pieces[0], preferred_element_type=jnp.float32)
    up_acc = jnp.einsum("tkcj,kcjh->tch", taken, pieces[1], preferred_element_type=jnp.float32)
    sig_gate = jax.nn.sigmoid(gate_acc)
    hidden = (gate_acc * sig_gate * up_acc).astype(jnp.bfloat16)
    upstream = grad_hidden.reshape(tok_rows, col_local, side).astype(jnp.float32)
    d_gate = (upstream * up_acc * sig_gate * (1.0 + gate_acc * (1.0 - sig_gate))).astype(
        jnp.bfloat16
    )
    d_up = (upstream * gate_acc * sig_gate).astype(jnp.bfloat16)
    pieces = (
        lax.all_gather(gate_blocks, "dp", axis=0, tiled=True),
        lax.all_gather(up_blocks, "dp", axis=0, tiled=True),
    )
    contrib = jnp.einsum("tch,kcjh->tkcj", d_gate, pieces[0], preferred_element_type=jnp.float32)
    grad_acc = jnp.einsum(
        "tkcj,kcr->trj",
        contrib + jnp.einsum("tch,kcjh->tkcj", d_up, pieces[1], preferred_element_type=jnp.float32),
        selector,
    )
    grad_inputs = lax.psum_scatter(
        grad_acc.reshape(tok_rows, row_blocks * side).astype(jnp.bfloat16),
        "tensor",
        scatter_dimension=1,
        tiled=True,
    )
    grad_scale = 1.0 / math.sqrt(tok_rows * lax.axis_size("dp"))
    rows_here = row_index
    taken = jnp.take(blocks, rows_here, axis=1)
    gate_term = jnp.einsum("tkcj,tch->kcjh", taken, d_gate, preferred_element_type=jnp.float32)
    up_term = jnp.einsum("tkcj,tch->kcjh", taken, d_up, preferred_element_type=jnp.float32)
    summed = lax.psum_scatter(
        (jnp.stack([gate_term, up_term], axis=1) * grad_scale).astype(jnp.bfloat16),
        "dp",
        scatter_dimension=0,
        tiled=True,
    ).astype(jnp.float32)
    grad_gate_blocks = summed[:, 0].astype(jnp.bfloat16)
    grad_up_blocks = summed[:, 1].astype(jnp.bfloat16)
    return (
        hidden.reshape(tok_rows, col_local * side),
        grad_inputs,
        grad_gate_blocks,
        grad_up_blocks,
    )


def solution(mesh):
    return jax.shard_map(
        per_device,
        mesh=mesh,
        in_specs=(
            P("dp", "tensor"),
            P("dp", "tensor", None, None),
            P("dp", "tensor", None, None),
            P(None, "tensor"),
            P("dp", "tensor"),
        ),
        out_specs=(
            P("dp", "tensor"),
            P("dp", "tensor"),
            P("dp", "tensor", None, None),
            P("dp", "tensor", None, None),
        ),
        check_vma=False,
    )
```

profile of v0, /device:TPU:8, one launch (start us, length us, event | category | flops | bytes accessed | tf_op | source)
XLA Modules:
  0.0 587.0 jit_solution(9665724028445907382)
XLA Ops:
  7.2 1.6 copy.71
  8.9 0.7 all-gather.8.cloned.1.call-update
  9.6 0.7 all-gather.6.cloned.1.call-update
  10.3 1.1 copy.77
  11.4 0.8 copy.68
  12.3 0.7 broadcast_compare_fusion
  13.0 0.2 select_reduce_fusion
  13.3 0.1 reshape.72
  13.5 0.1 copy.70
  13.6 79.3 %all-gather.4.cloned.1.call-done = bf16[128,4096]{0,1:T(8,128)(2,1)} async-done(((bf16[128,256]{0,1:T(8,128)(2,1)}), bf16[128,4096]{0,1:T(8,128)(2,1)}) %all-gather.4.cloned.1.call-update) | async-done | bytes 1048592 | tf_op jit(solution)/shard_map/all_gather | solution.py:24
  92.9 1.6 copy.73
  94.5 2.9 gather_fusion
  97.4 32.6 %all-gather.8.cloned.1.call-done = bf16[16,7,128,128]{3,2,1,0:T(8,128)(2,1)} async-done(((bf16[1,7,128,128]{3,2,1,0:T(8,128)(2,1)}), bf16[16,7,128,128]{3,2,1,0:T(8,128)(2,1)}) %all-gather.8.cloned.1.call-update) | async-done | bytes 3670032 | tf_op jit(solution)/shard_map/all_gather | solution.py:29
  130.0 4.6 convolution_bitcast_fusion
  134.6 36.6 %all-gather.6.cloned.1.call-done = bf16[16,7,128,128]{3,2,1,0:T(8,128)(2,1)} async-done(((bf16[1,7,128,128]{3,2,1,0:T(8,128)(2,1)}), bf16[16,7,128,128]{3,2,1,0:T(8,128)(2,1)}) %all-gather.6.cloned.1.call-update) | async-done | bytes 3670032 | tf_op jit(solution)/shard_map/all_gather | solution.py:28
  171.3 4.9 multiply_convert_fusion.1
  176.1 4.2 fusion.14
  180.4 4.1 fusion.11
  184.5 10.2 %fusion = bf16[16,2,7,128,128]{3,4,0,2,1:T(8,128)(2,1)} fusion(f32[16,1,7,128,128]{3,4,0,2,1:T(8,128)} %fusion.14, f32[16,1,7,128,128]{3,4,0,2,1:T(8,128)} %fusion.11), kind=kLoop, calls=%fused_computation.2 | loop fusion | flops 11010048 | bytes 22020096 | tf_op jit(solution)/shard_map/convert_element_type | solution.py:64
  194.7 0.2 reduce-scatter.5.cloned.1.call-start
  195.0 0.4 copy-done.2
  195.4 3.3 fusion.3
  198.7 1.2 add_bitcast_fusion
  199.9 2.4 bitcast_convert_fusion
  202.3 1.4 copy.121
  203.8 0.6 dynamic-slice
  204.3 0.8 copy.85
  205.2 167.0 %all-reduce.3.cloned.1.call-done = bf16[16,2,7,128,128]{3,4,0,2,1:T(8,128)(2,1)} async-done(((bf16[16,2,7,128,128]{3,4,0,2,1:T(8,128)(2,1)}), bf16[16,2,7,128,128]{3,4,0,2,1:T(8,128)(2,1)}) %all-reduce.3.cloned.1.call-update) | async-done | bytes 7340048
  372.2 1.7 dynamic-slice_bitcast_fusion
  373.9 0.8 copy.86
  374.8 0.8 copy.87
  375.6 204.9 %reduce-scatter.5.cloned.1.call-done = bf16[128,256]{1,0:T(8,128)(2,1)} async-done(((bf16[128,4096]{1,0:T(8,128)(2,1)}), bf16[128,256]{1,0:T(8,128)(2,1)}) %reduce-scatter.5.cloned.1.call-update) | async-done | bytes 65552 | tf_op jit(solution)/shard_map/reduce_scatter | solution.py:52
  (23 shorter events, 0.5 us)
Async XLA Ops:
  7.2 85.7 %all-gather.4.cloned.1.call-start = ((), (), s32[]{:S(2)}) async-start(), calls=%async_computation.1 | async-start | bytes 1114112 | tf_op jit(solution)/shard_map/all_gather | solution.py:24
  8.8 121.2 %all-gather.8.cloned.1.call-start = ((), (), s32[]{:S(2)}) async-start(), calls=%async_computation.3 | async-start | bytes 3899392 | tf_op jit(solution)/shard_map/all_gather | solution.py:29
  9.6 161.7 %all-gather.6.cloned.1.call-start = ((), (), s32[]{:S(2)}) async-start(), calls=%async_computation.2 | async-start | bytes 3899392 | tf_op jit(solution)/shard_map/all_gather | solution.py:28
  10.3 361.9 %all-reduce.3.cloned.1.call-start = ((), (), s32[]{:S(2)}) async-start(), calls=%async_computation.5 | async-start | bytes 14680064
  171.3 4.9 copy-start
  194.7 0.7 copy-start.2
  194.7 385.8 %reduce-scatter.5.cloned.1.call-start = ((), (), s32[]{:S(2)}) async-start(), calls=%async_computation.4 | async-start | bytes 1114112 | tf_op jit(solution)/shard_map/reduce_scatter | solution.py:52
  195.4 3.4 copy-start.1
  199.9 3.8 copy-start.3
Sparse Core Ops, SparseCore 0:
  11.2 81.6 all-gather.3
  94.7 35.2 all-gather.7
  131.9 39.3 all-gather.5
  194.8 177.3 all-reduce.2
  376.4 203.9 reduce-scatter.4
where the time goes:
time: 587 us
  waiting for transfers between devices  522 us (89%)
  matrix products  24.7 us (4%)
  local copies, waits for them, and re-layouts  14.9 us (3%)
  between operations  13.9 us (2%)
  other arithmetic  11.2 us (2%)
    reduce_scatter x1, waiting for transfers between devices, per_device(): lax.psum_scatter(grad_acc.reshape(tok_rows, row_blocks * side).astype(jnp...  205 us
    unnamed x6, waiting for transfers between devices  168 us
    all_gather x1, waiting for transfers between devices, per_device(): whole = lax.all_gather(inputs, 'tensor', axis=1, tiled=True)  79.3 us
    all_gather x1, waiting for transfers between devices, per_device(): lax.all_gather(gate_blocks, 'dp', axis=0, tiled=True)  36.6 us
    all_gather x1, waiting for transfers between devices, per_device(): lax.all_gather(up_blocks, 'dp', axis=0, tiled=True)  32.6 us
  transfers between devices with their start and end apart: 5, of which 5 were waited for; matrix products, arithmetic and copies ran while one was open for 4% of the time, Pallas kernels for 0%

commit v1 on v0

--- a/solution.py
+++ b/solution.py
@@ -26,7 +26,9 @@
     blocks = whole.reshape(tok_rows, row_blocks, side)
     pieces = (
         lax.all_gather(gate_blocks, "dp", axis=0, tiled=True),
-        lax.all_gather(up_blocks, "dp", axis=0, tiled=True),
+        jnp.concatenate(
+            lax.all_to_all(jnp.stack([up_blocks] * lax.axis_size("dp")), "dp", 0, 0), axis=0
+        ),
     )
     rows_here = row_index
     taken = jnp.take(blocks, rows_here, axis=1)

time: 587 us -> 567 us (0.966)
  waiting for transfers between devices: 522 us -> 493 us
  starting transfers between devices: 0.38 us -> 6.96 us
    all_gather x1, waiting for transfers between devices: 32.6 us -> 17.2 us  [per_device(): lax.all_gather(up_blocks, 'dp', axis=0, tiled=True)]
    all_gather x1, waiting for transfers between devices: 36.6 us -> 28.5 us  [per_device(): lax.all_gather(gate_blocks, 'dp', axis=0, tiled=True)]
    all_gather x1, waiting for transfers between devices: 79.3 us -> 71.3 us  [per_device(): whole = lax.all_gather(inputs, 'tensor', axis=1, tiled=True)]
    all_to_all x0 -> x1, starting transfers between devices: none -> 6.59 us  [per_device(): lax.all_to_all(jnp.stack([up_blocks] * lax.axis_size('dp')), 'dp', 0, 0)]
  transfers between devices with their start and end apart: 5 -> 6, of which waited for: 5 -> 5; matrix products, arithmetic and copies ran while one was open for 4% -> 9% of each run, Pallas kernels for 0% -> 0%
where the time goes in v1:
time: 567 us; the launch traced here: 566 us
  waiting for transfers between devices  493 us (87%)
  matrix products  24.4 us (4%)
  local copies, waits for them, and re-layouts  16.9 us (3%)
  between operations  13.9 us (2%)
  other arithmetic  10.7 us (2%)
  starting transfers between devices  6.96 us (1%)
    reduce_scatter x1, waiting for transfers between devices, per_device(): lax.psum_scatter(grad_acc.reshape(tok_rows, row_blocks * side).astype(jnp...  205 us
    unnamed x6, waiting for transfers between devices  171 us
    all_gather x1, waiting for transfers between devices, per_device(): whole = lax.all_gather(inputs, 'tensor', axis=1, tiled=True)  71.3 us
    all_gather x1, waiting for transfers between devices, per_device(): lax.all_gather(gate_blocks, 'dp', axis=0, tiled=True)  28.5 us
    all_gather x1, waiting for transfers between devices, per_device(): lax.all_gather(up_blocks, 'dp', axis=0, tiled=True)  17.2 us
  transfers between devices with their start and end apart: 6, of which 5 were waited for; matrix products, arithmetic and copies ran while one was open for 9% of the time, Pallas kernels for 0%

profile of v1, /device:TPU:8, one launch (start us, length us, event | category | flops | bytes accessed | tf_op | source)
XLA Modules:
  0.0 566.5 jit_solution(1044685857711189286)
XLA Ops:
  7.2 1.6 copy.71
  8.9 0.7 all-gather.6.cloned.1.call-update
  9.6 0.7 all-gather.8.cloned.1.call-update
  10.3 1.1 copy.75
  11.4 2.8 stack.8
  14.2 6.6 %all-to-all-start = ((bf16[16,1,7,128,128]{3,4,2,1,0:T(8,128)(2,1)}), bf16[16,1,7,128,128]{3,4,2,1,0:T(8,128)(2,1)}, u32[]{:S(2)}, u32[]{:S(2)}) async-start(bf16[16,1,7,128,128]{3,4,2,1,0:T(8,128)(2,1)} %stack.8), calls=%async_computation | async-start | bytes 7340032 | tf_op jit(solution)/shard_map/all_to_all | solution.py:30
  20.8 0.1 copy.77
  21.2 0.2 select_reduce_fusion
  21.5 0.1 reshape.79
  21.6 0.1 copy.70
  21.7 71.3 %all-gather.4.cloned.1.call-done = bf16[128,4096]{0,1:T(8,128)(2,1)} async-done(((bf16[128,256]{0,1:T(8,128)(2,1)}), bf16[128,4096]{0,1:T(8,128)(2,1)}) %all-gather.4.cloned.1.call-update) | async-done | bytes 1048592 | tf_op jit(solution)/shard_map/all_gather | solution.py:24
  93.1 1.6 copy.73
  94.7 3.0 gather_fusion
  97.7 4.4 fusion.21
  102.0 28.5 %all-gather.6.cloned.1.call-done = bf16[16,7,128,128]{3,2,1,0:T(8,128)(2,1)} async-done(((bf16[1,7,128,128]{3,2,1,0:T(8,128)(2,1)}), bf16[16,7,128,128]{3,2,1,0:T(8,128)(2,1)}) %all-gather.6.cloned.1.call-update) | async-done | bytes 3670032 | tf_op jit(solution)/shard_map/all_gather | solution.py:28
  130.5 4.9 multiply_convert_fusion.1
  135.4 4.2 fusion.14
  139.6 4.1 fusion.11
  143.7 10.4 %fusion = bf16[16,2,7,128,128]{3,4,0,2,1:T(8,128)(2,1)} fusion(f32[16,1,7,128,128]{3,4,0,2,1:T(8,128)} %fusion.14, f32[16,1,7,128,128]{3,4,0,2,1:T(8,128)} %fusion.11), kind=kLoop, calls=%fused_computation.2 | loop fusion | flops 11010048 | bytes 22020096 | tf_op jit(solution)/shard_map/convert_element_type | solution.py:66
  154.2 0.2 reduce-scatter.5.cloned.1.call-start
  154.5 17.2 %all-gather.8.cloned.1.call-done = bf16[16,7,128,128]{3,2,0,1:T(8,128)(2,1)} async-done(((bf16[1,7,128,128]{3,2,0,1:T(8,128)(2,1)}), bf16[16,7,128,128]{3,2,0,1:T(8,128)(2,1)}) %all-gather.8.cloned.1.call-update) | async-done | bytes 3670032 | tf_op jit(solution)/shard_map/all_gather | solution.py:46
  171.7 3.3 fusion.25
  175.1 1.2 add_bitcast_fusion
  176.2 2.4 bitcast_convert_fusion
  178.6 1.4 copy.118
  180.1 0.6 dynamic-slice
  180.7 0.8 copy.85
  181.5 170.1 %all-reduce.3.cloned.1.call-done = bf16[16,2,7,128,128]{3,4,0,2,1:T(8,128)(2,1)} async-done(((bf16[16,2,7,128,128]{3,4,0,2,1:T(8,128)(2,1)}), bf16[16,2,7,128,128]{3,4,0,2,1:T(8,128)(2,1)}) %all-reduce.3.cloned.1.call-update) | async-done | bytes 7340048
  351.6 1.7 dynamic-slice_bitcast_fusion
  353.3 0.8 copy.86
  354.1 0.8 copy.87
  355.0 204.9 %reduce-scatter.5.cloned.1.call-done = bf16[128,256]{1,0:T(8,128)(2,1)} async-done(((bf16[128,4096]{1,0:T(8,128)(2,1)}), bf16[128,256]{1,0:T(8,128)(2,1)}) %reduce-scatter.5.cloned.1.call-update) | async-done | bytes 65552 | tf_op jit(solution)/shard_map/reduce_scatter | solution.py:54
  (29 shorter events, 0.6 us)
Async XLA Ops:
  7.2 85.9 %all-gather.4.cloned.1.call-start = ((), (), s32[]{:S(2)}) async-start(), calls=%async_computation.2 | async-start | bytes 1114112 | tf_op jit(solution)/shard_map/all_gather | solution.py:24
  8.8 121.7 %all-gather.6.cloned.1.call-start = ((), (), s32[]{:S(2)}) async-start(), calls=%async_computation.3 | async-start | bytes 3899392 | tf_op jit(solution)/shard_map/all_gather | solution.py:28
  9.6 162.1 %all-gather.8.cloned.1.call-start = ((), (), s32[]{:S(2)}) async-start(), calls=%async_computation.4 | async-start | bytes 3899392 | tf_op jit(solution)/shard_map/all_gather | solution.py:46
  14.2 6.6 %copy-start.2 = (bf16[128,896]{1,0:T(8,128)(2,1)S(1)}, bf16[128,896]{1,0:T(8,128)(2,1)}, u32[]{:S(2)}) copy-start(bf16[128,896]{1,0:T(8,128)(2,1)} %param.11) | copy-start | bytes 688132
  14.2 6.8 %copy-start.3 = (s32[32,7]{0,1:T(8,128)S(1)}, s32[32,7]{0,1:T(8,128)}, u32[]{:S(2)}) copy-start(s32[32,7]{0,1:T(8,128)} %param.10) | copy-start | bytes 2692
  14.2 83.5 %all-to-all-start = ((bf16[16,1,7,128,128]{3,4,2,1,0:T(8,128)(2,1)}), bf16[16,1,7,128,128]{3,4,2,1,0:T(8,128)(2,1)}, u32[]{:S(2)}, u32[]{:S(2)}) async-start(bf16[16,1,7,128,128]{3,4,2,1,0:T(8,128)(2,1)} %stack.8), calls=%async_computation | async-start | bytes 7340032 | tf_op jit(solution)/shard_map/all_to_all | solution.py:30
  20.8 330.8 %all-reduce.3.cloned.1.call-start = ((), (), s32[]{:S(2)}) async-start(), calls=%async_computation.6 | async-start | bytes 14680064
  130.5 4.9 copy-start
  154.2 405.8 %reduce-scatter.5.cloned.1.call-start = ((), (), s32[]{:S(2)}) async-start(), calls=%async_computation.5 | async-start | bytes 1114112 | tf_op jit(solution)/shard_map/reduce_scatter | solution.py:54
  171.7 3.4 copy-start.1
  176.2 3.9 copy-start.4
Sparse Core Ops, SparseCore 0:
  11.2 81.8 all-gather.3
  94.9 35.5 all-gather.5
  132.3 39.3 all-gather.7
  174.2 177.3 all-reduce.2
  355.8 204.0 reduce-scatter.4
